TPU v7x, 32 devices: a whole 2x2x4 slice. The times are simulated.
32 devices in a mesh: grp: 2 (over y), row: 4 (over z), col: 2 (over x), pair: 2 (over core).
Axes of the slice: x: 2, y: 2, z: 4, core: 2. Of those that a mesh axis runs over, the one named last changes fastest.
Arguments:
- features_in: bfloat16 [128, 32, 512], P('grp', 'row', ('col', 'pair')), parts along dimension 0, may hold values from -8 to 8
- filters_one: bfloat16 [64, 3, 3, 64], replicated, may hold values from -0.25 to 0.25
- filters_two: bfloat16 [512, 3, 3, 256], P('row'), may hold values from -0.125 to 0.125
- out_grad: bfloat16 [1024, 128, 8], P(('grp', 'row'), ('col', 'pair')), parts along dimension 0, may hold values from -24 to 24
Outputs:
- input_grad: bfloat16 [128, 32, 512], P('grp', 'row', ('col', 'pair')), parts along dimension 0
- grad_one: float32 [128, 3, 3, 64], P('grp'), parts along dimension 0
- grad_two: float32 [1024, 3, 3, 256], P(('grp', 'row')), parts along dimension 0
There are 2 independent parts, one for each index of `grp`. A program takes and returns all parts, laid end to end along the dimension named above; an argument that names none is the same for every part. Nothing has to cross between parts.
All inputs are finite; a program needn't handle non-finite values.
Results may differ from a plain program's by a relative error of at most 0.015.
Values may be sent and summed in bfloat16 or wider, within the bound.
A program may use at most 64 MiB of HBM per device.

v0:
```python
import math
import jax
import jax.numpy as jnp
from jax import lax
from jax.sharding import PartitionSpec as P


def padded_2(cells, sides, width):
    for axis, dim in sides:
        count = lax.axis_size(axis)
        ends = count - 1
        head = lax.slice_in_dim(cells, 0, width, axis=dim)
        tail = lax.slice_in_dim(cells, cells.shape[dim] - width, cells.shape[dim], axis=dim)
        cells = jnp.concatenate(
            [
                lax.ppermute(tail, axis, [(i, (i + 1) % count) for i in range(ends)]),
                cells,
                lax.ppermute(head, axis, [((i + 1) % count, i) for i in range(ends)]),
            ],
            axis=dim,
        )
    return cells


def conv_valid(padded, kernel):
    return lax.conv_general_dilated(
        padded[None],
        kernel,
        (1, 1),
        "VALID",
        dimension_numbers=("NCHW", "OHWI", "NCHW"),
        preferred_element_type=jnp.float32,
    )[0]


def flip_kernel(kernel):
    return jnp.transpose(kernel[:, ::-1, ::-1, :], (3, 1, 2, 0))


def silu_slope(values):
    sigmoid_value = jax.nn.sigmoid(values)
    return sigmoid_value * (1.0 + values * (1.0 - sigmoid_value))


def tap_grads(gradient, padded):
    row_count, col_count = (gradient.shape[1], gradient.shape[2])
    tap_list = []
    for first_tap in range(3):
        tap_row = []
        for second_tap in range(3):
            window = padded[
                :, first_tap : first_tap + row_count, second_tap : second_tap + col_count
            ]
            tap_row.append(
                jnp.einsum("ohw,chw->oc", gradient, window, preferred_element_type=jnp.float32)
            )
        tap_list.append(jnp.stack(tap_row, 1))
    return jnp.stack(tap_list, 1)


def pool_columns(active):
    channels, row_count, col_count = active.shape
    folded = active.reshape(channels, row_count // 4, 2, 2, col_count // 4, 2, 2).mean(axis=(3, 6))
    return jnp.transpose(folded, (0, 2, 4, 3, 1)).reshape(
        channels * 4, col_count // 4, row_count // 4
    )


def unpool_columns(gradient):
    quad_count, col_count, row_count = gradient.shape
    ordered = jnp.transpose(
        gradient.reshape(quad_count // 4, 2, 2, col_count, row_count), (0, 4, 1, 3, 2)
    )
    spread = (
        jnp.broadcast_to(
            ordered[:, :, :, None, :, :, None], (quad_count // 4, row_count, 2, 2, col_count, 2, 2)
        )
        * 0.25
    )
    return spread.reshape(quad_count // 4, row_count * 4, col_count * 4)


def local(features_in, filters_one, filters_two, out_grad):
    band_rows = features_in.shape[1]
    strip_cols = features_in.shape[2]
    height = band_rows * lax.axis_size("row")
    width = strip_cols * lax.axis_size(("col", "pair"))
    padded_in = padded_2(features_in, (("row", 1), (("col", "pair"), 2)), 1)
    pre_one = conv_valid(padded_in, filters_one)
    pooled = pool_columns(jax.nn.silu(pre_one)).astype(jnp.bfloat16)
    with_edges = padded_2(pooled, ((("col", "pair"), 1),), 1)
    column_strip = lax.all_gather(with_edges, "row", axis=2, tiled=True)
    strip_padded = jnp.pad(column_strip, ((0, 0), (0, 0), (1, 1)))
    swapped = jnp.transpose(filters_two, (0, 2, 1, 3))
    pre_two = conv_valid(strip_padded, swapped)
    grad_pre_two = (out_grad.astype(jnp.float32) * silu_slope(pre_two)).astype(jnp.bfloat16)
    pooled_height = column_strip.shape[2]
    pooled_width = strip_cols // 4 * lax.axis_size(("col", "pair"))
    local_two = jnp.transpose(tap_grads(grad_pre_two, strip_padded), (0, 2, 1, 3))
    grad_two = lax.psum(local_two, ("col", "pair")) / math.sqrt(pooled_height * pooled_width)
    padded_grad = jnp.pad(grad_pre_two, ((0, 0), (2, 2), (1, 1)))
    spread_grad = conv_valid(padded_grad, flip_kernel(swapped))
    with_ghosts = padded_2(spread_grad, ((("col", "pair"), 1),), 1)
    real_columns = spread_grad[:, 1:-1, :]
    real_columns = real_columns.at[:, 0, :].add(with_ghosts[:, 0, :])
    real_columns = real_columns.at[:, -1, :].add(with_ghosts[:, -1, :])
    grad_pooled = lax.psum_scatter(real_columns, "row", scatter_dimension=2, tiled=True)
    grad_pre_one = (unpool_columns(grad_pooled) * silu_slope(pre_one)).astype(jnp.bfloat16)
    local_one = tap_grads(grad_pre_one, padded_in)
    grad_one = lax.psum(local_one, ("row", "col", "pair")) / math.sqrt(height * width)
    rimmed_one = padded_2(grad_pre_one, (("row", 1), (("col", "pair"), 2)), 1)
    input_grad = conv_valid(rimmed_one, flip_kernel(filters_one)).astype(jnp.bfloat16)
    return (input_grad, grad_one, grad_two)


def solution(mesh):
    in_specs = (
        P("grp", "row", ("col", "pair")),
        P(),
        P("row", None, None, None),
        P(("grp", "row"), ("col", "pair"), None),
    )
    out_specs = (
        P("grp", "row", ("col", "pair")),
        P("grp", None, None, None),
        P(("grp", "row"), None, None, None),
    )
    return jax.shard_map(local, mesh=mesh, in_specs=in_specs, out_specs=out_specs, check_vma=False)
```

profile of v0, /device:TPU:0, one launch (start us, length us, event | category | flops | bytes accessed | tf_op | source)
XLA Modules:
  0.0 211.8 jit_solution(14888131075437018906)
XLA Ops:
  8.1 1.0 copy.216
  9.1 4.9 %collective-permute-start = (bf16[64,1,128]{2,0,1:T(8,128)(2,1)S(1)}, bf16[64,1,128]{2,0,1:T(8,128)(2,1)S(1)}, u32[]{:S(2)}, u32[]{:S(2)}) collective-permute-start(bf16[64,1,128]{2,0,1:T(8,128)(2,1)S(1)} %get-tuple-element.58), channel_id=1, source_target_pairs={{0,4},{4,8},{8,12},{1,5},{5,9},{9,13},{2,6},{6,10},{10,14},{3,7},{... | collective-permute-start | bytes 49160 | tf_op jit(solution)/shard_map/ppermute | solution.py:16
  14.0 1.3 collective-permute-start.1
  15.4 0.9 constant_dynamic-update-slice_fusion.1
  16.4 3.3 %collective-permute-done.1 = bf16[64,1,128]{2,0,1:T(8,128)(2,1)S(1)} collective-permute-done((bf16[64,1,128]{2,0,1:T(8,128)(2,1)S(1)}, bf16[64,1,128]{2,0,1:T(8,128)(2,1)S(1)}, u32[]{:S(2)}, u32[]{:S(2)}) %collective-permute-start.1) | collective-permute-done | bytes 16416 | tf_op jit(solution)/shard_map/ppermute | solution.py:18
  19.7 1.3 collective-permute-start.3
  21.0 3.0 %collective-permute-start.2 = (bf16[64,10,1]{2,0,1:T(8,128)(2,1)S(1)}, bf16[64,10,1]{2,0,1:T(8,128)(2,1)S(1)}, u32[]{:S(2)}, u32[]{:S(2)}) collective-permute-start(bf16[64,10,1]{2,0,1:T(8,128)(2,1)S(1)} %get-tuple-element.51), channel_id=1, source_target_pairs={{0,1},{1,2},{2,3},{4,5},{5,6},{6,7},{8,9},{9,10},{10,11},{12,13},{... | collective-permute-start | bytes 3848 | tf_op jit(solution)/shard_map/ppermute | solution.py:16
  24.1 1.0 collective-permute-done.2
  25.3 0.3 copy.265
  25.9 0.6 copy-done.3
  26.5 0.8 convolution_select_fusion.1
  27.6 0.9 fusion.3
  28.8 1.3 collective-permute-start.5
  30.1 4.9 %collective-permute-start.4 = (bf16[256,1,2]{1,0,2:T(8,128)(2,1)S(1)}, bf16[256,1,2]{1,0,2:T(8,128)(2,1)S(1)}, u32[]{:S(2)}, u32[]{:S(2)}) collective-permute-start(bf16[256,1,2]{1,0,2:T(8,128)(2,1)S(1)} %get-tuple-element.55), channel_id=1, source_target_pairs={{0,1},{1,2},{2,3},{4,5},{5,6},{6,7},{8,9},{9,10},{10,11},{12,13},{... | collective-permute-start | bytes 3080 | tf_op jit(solution)/shard_map/ppermute | solution.py:16
  35.0 0.2 copy.264
  35.3 0.7 collective-permute-done.4
  36.2 13.7 %all_gather.3 = bf16[256,34,8]{0,1,2:T(8,128)(2,1)S(1)} all-gather(bf16[256,34,2]{0,1,2:T(8,128)(2,1)S(1)} %copy.226), channel_id=1, replica_groups=mesh['grp'=2,'row'=4,'col'=2,'pair'=2] {'row'}, dimensions={2}, use_global_device_ids=true | all-gather | bytes 174080 | tf_op jit(solution)/shard_map/all_gather | solution.py:92
  50.1 1.0 fusion.6
  52.8 1.0 fusion.4
  53.9 2.4 %collective-permute-start.6 = (f32[256,1,8]{0,2,1:T(8,128)S(1)}, f32[256,1,8]{0,2,1:T(8,128)S(1)}, u32[]{:S(2)}, u32[]{:S(2)}) collective-permute-start(f32[256,1,8]{0,2,1:T(8,128)S(1)} %get-tuple-element.48), channel_id=1, source_target_pairs={{0,1},{1,2},{2,3},{4,5},{5,6},{6,7},{8,9},{9,10},{10,11},{12,13},{... | collective-permute-start | bytes 24584 | tf_op jit(solution)/shard_map/ppermute | solution.py:16
  56.6 1.3 collective-permute-start.7
  57.9 6.6 %collective-permute-done.7 = f32[256,1,8]{0,2,1:T(8,128)S(1)} collective-permute-done((f32[256,1,8]{0,2,1:T(8,128)S(1)}, f32[256,1,8]{0,2,1:T(8,128)S(1)}, u32[]{:S(2)}, u32[]{:S(2)}) %collective-permute-start.7) | collective-permute-done | bytes 8224 | tf_op jit(solution)/shard_map/ppermute | solution.py:18
  64.4 0.8 copy.233
  65.7 1.1 maximum_bitcast_fusion
  66.8 18.7 %reduce-scatter.2.cloned.1.call-done = f32[256,32,2]{0,1,2:T(8,128)} async-done(((f32[256,32,8]{0,1,2:T(8,128)}), f32[256,32,2]{0,1,2:T(8,128)}) %reduce-scatter.2.cloned.1.call-update) | async-done | bytes 65552 | tf_op jit(solution)/shard_map/reduce_scatter | solution.py:107
  85.5 0.8 broadcast_multiply_fusion.2
  87.1 0.4 copy-done.1
  87.7 1.3 collective-permute-start.8
  89.0 1.3 collective-permute-start.9
  90.3 0.3 convolution_bitcast_fusion.15
  90.8 0.3 convolution_bitcast_fusion.17
  91.0 0.3 convolution_bitcast_fusion.12
  91.3 0.3 convolution_bitcast_fusion.14
  91.6 0.3 convolution_bitcast_fusion.9
  92.0 0.2 convolution_bitcast_fusion.11
  92.4 2.4 %collective-permute-done.9 = bf16[64,1,128]{2,1,0:T(2,128)(2,1)S(1)} collective-permute-done((bf16[64,1,128]{2,1,0:T(2,128)(2,1)S(1)}, bf16[64,1,128]{2,1,0:T(2,128)(2,1)S(1)}, u32[]{:S(2)}, u32[]{:S(2)}) %collective-permute-start.9) | collective-permute-done | bytes 16416 | tf_op jit(solution)/shard_map/ppermute | solution.py:18
  94.9 1.3 collective-permute-start.11
  96.2 3.0 %collective-permute-start.10 = (bf16[64,10,1]{2,0,1:T(8,128)(2,1)S(1)}, bf16[64,10,1]{2,0,1:T(8,128)(2,1)S(1)}, u32[]{:S(2)}, u32[]{:S(2)}) collective-permute-start(bf16[64,10,1]{2,0,1:T(8,128)(2,1)S(1)} %get-tuple-element.49), channel_id=1, source_target_pairs={{0,1},{1,2},{2,3},{4,5},{5,6},{6,7},{8,9},{9,10},{10,11},{12,13},{... | collective-permute-start | bytes 3848 | tf_op jit(solution)/shard_map/ppermute | solution.py:16
  99.3 0.7 pad_maximum_fusion
  100.0 0.2 collective-permute-done.10
  100.5 0.3 copy.266
  101.0 0.6 fusion
  101.7 0.9 copy.259
  102.6 5.7 %all-reduce.7.cloned.1.call-done = f32[128,3,3,256]{3,0,1,2:T(8,128)} async-done(((f32[128,3,3,256]{3,0,1,2:T(8,128)}), f32[128,3,3,256]{3,0,1,2:T(8,128)}) %all-reduce.7.cloned.1.call-update) | async-done | bytes 1179664 | tf_op jit(solution)/shard_map/psum | solution.py:100
  108.3 1.4 broadcast_multiply_fusion
  109.7 1.1 copy.260
  110.8 91.9 %all-reduce.5.cloned.1.call-done = f32[64,3,3,64]{3,0,2,1:T(8,128)} async-done(((f32[64,3,3,64]{3,0,2,1:T(8,128)}), f32[64,3,3,64]{3,0,2,1:T(8,128)}) %all-reduce.5.cloned.1.call-update) | async-done | bytes 147472 | tf_op jit(solution)/shard_map/psum | solution.py:110
  202.6 1.7 broadcast_multiply_fusion.1
  (79 shorter events, 6.1 us)
Async XLA Ops:
  8.0 42.1 %copy-start = (bf16[128,3,3,256]{3,0,2,1:T(8,128)(2,1)S(1)}, bf16[128,3,3,256]{3,0,2,1:T(8,128)(2,1)}, u32[]{:S(2)}) copy-start(bf16[128,3,3,256]{3,0,2,1:T(8,128)(2,1)} %param.10) | copy-start | bytes 1769476
  8.0 77.5 %reduce-scatter.2.cloned.1.call-start = ((), (), s32[]{:S(2)}) async-start(), calls=%async_computation.1 | async-start | bytes 327680 | tf_op jit(solution)/shard_map/reduce_scatter | solution.py:107
  9.1 6.4 %collective-permute-start = (bf16[64,1,128]{2,0,1:T(8,128)(2,1)S(1)}, bf16[64,1,128]{2,0,1:T(8,128)(2,1)S(1)}, u32[]{:S(2)}, u32[]{:S(2)}) collective-permute-start(bf16[64,1,128]{2,0,1:T(8,128)(2,1)S(1)} %get-tuple-element.58), channel_id=1, source_target_pairs={{0,4},{4,8},{8,12},{1,5},{5,9},{9,13},{2,6},{6,10},{10,14},{3,7},{... | collective-permute-start | bytes 49160 | tf_op jit(solution)/shard_map/ppermute | solution.py:16
  14.0 5.6 %collective-permute-start.1 = (bf16[64,1,128]{2,0,1:T(8,128)(2,1)S(1)}, bf16[64,1,128]{2,0,1:T(8,128)(2,1)S(1)}, u32[]{:S(2)}, u32[]{:S(2)}) collective-permute-start(bf16[64,1,128]{2,0,1:T(8,128)(2,1)S(1)} %get-tuple-element.57), channel_id=1, source_target_pairs={{4,0},{8,4},{12,8},{5,1},{9,5},{13,9},{6,2},{10,6},{14,10},{7,3},{... | collective-permute-start | bytes 49160 | tf_op jit(solution)/shard_map/ppermute | solution.py:18
  19.7 4.4 %collective-permute-start.3 = (bf16[64,10,1]{2,0,1:T(8,128)(2,1)S(1)}, bf16[64,10,1]{2,0,1:T(8,128)(2,1)S(1)}, u32[]{:S(2)}, u32[]{:S(2)}) collective-permute-start(bf16[64,10,1]{2,0,1:T(8,128)(2,1)S(1)} %get-tuple-element.52), channel_id=1, source_target_pairs={{1,0},{2,1},{3,2},{5,4},{6,5},{7,6},{9,8},{10,9},{11,10},{13,12},{... | collective-permute-start | bytes 3848 | tf_op jit(solution)/shard_map/ppermute | solution.py:18
  21.0 4.0 %collective-permute-start.2 = (bf16[64,10,1]{2,0,1:T(8,128)(2,1)S(1)}, bf16[64,10,1]{2,0,1:T(8,128)(2,1)S(1)}, u32[]{:S(2)}, u32[]{:S(2)}) collective-permute-start(bf16[64,10,1]{2,0,1:T(8,128)(2,1)S(1)} %get-tuple-element.51), channel_id=1, source_target_pairs={{0,1},{1,2},{2,3},{4,5},{5,6},{6,7},{8,9},{9,10},{10,11},{12,13},{... | collective-permute-start | bytes 3848 | tf_op jit(solution)/shard_map/ppermute | solution.py:16
  25.6 0.9 copy-start.3
  25.6 0.9 copy-start.4
  28.8 6.4 %collective-permute-start.5 = (bf16[256,1,2]{1,0,2:T(8,128)(2,1)S(1)}, bf16[256,1,2]{1,0,2:T(8,128)(2,1)S(1)}, u32[]{:S(2)}, u32[]{:S(2)}) collective-permute-start(bf16[256,1,2]{1,0,2:T(8,128)(2,1)S(1)} %get-tuple-element.56), channel_id=1, source_target_pairs={{1,0},{2,1},{3,2},{5,4},{6,5},{7,6},{9,8},{10,9},{11,10},{13,12},{... | collective-permute-start | bytes 3080 | tf_op jit(solution)/shard_map/ppermute | solution.py:18
  30.1 5.9 %collective-permute-start.4 = (bf16[256,1,2]{1,0,2:T(8,128)(2,1)S(1)}, bf16[256,1,2]{1,0,2:T(8,128)(2,1)S(1)}, u32[]{:S(2)}, u32[]{:S(2)}) collective-permute-start(bf16[256,1,2]{1,0,2:T(8,128)(2,1)S(1)} %get-tuple-element.55), channel_id=1, source_target_pairs={{0,1},{1,2},{2,3},{4,5},{5,6},{6,7},{8,9},{9,10},{10,11},{12,13},{... | collective-permute-start | bytes 3080 | tf_op jit(solution)/shard_map/ppermute | solution.py:16
  50.1 1.0 copy-start.2
  53.9 4.0 %collective-permute-start.6 = (f32[256,1,8]{0,2,1:T(8,128)S(1)}, f32[256,1,8]{0,2,1:T(8,128)S(1)}, u32[]{:S(2)}, u32[]{:S(2)}) collective-permute-start(f32[256,1,8]{0,2,1:T(8,128)S(1)} %get-tuple-element.48), channel_id=1, source_target_pairs={{0,1},{1,2},{2,3},{4,5},{5,6},{6,7},{8,9},{9,10},{10,11},{12,13},{... | collective-permute-start | bytes 24584 | tf_op jit(solution)/shard_map/ppermute | solution.py:16
  56.6 7.9 %collective-permute-start.7 = (f32[256,1,8]{0,2,1:T(8,128)S(1)}, f32[256,1,8]{0,2,1:T(8,128)S(1)}, u32[]{:S(2)}, u32[]{:S(2)}) collective-permute-start(f32[256,1,8]{0,2,1:T(8,128)S(1)} %get-tuple-element.47), channel_id=1, source_target_pairs={{1,0},{2,1},{3,2},{5,4},{6,5},{7,6},{9,8},{10,9},{11,10},{13,12},{... | collective-permute-start | bytes 24584 | tf_op jit(solution)/shard_map/ppermute | solution.py:18
  65.3 43.0 %all-reduce.7.cloned.1.call-start = ((), (), s32[]{:S(2)}) async-start(), calls=%async_computation.3 | async-start | bytes 2359296 | tf_op jit(solution)/shard_map/psum | solution.py:100
  66.8 135.9 %all-reduce.5.cloned.1.call-start = ((), (), s32[]{:S(2)}) async-start(), calls=%async_computation.2 | async-start | bytes 589824 | tf_op jit(solution)/shard_map/psum | solution.py:110
  86.6 0.9 copy-start.1
  87.7 4.6 %collective-permute-start.8 = (bf16[64,1,128]{2,1,0:T(2,128)(2,1)S(1)}, bf16[64,1,128]{2,1,0:T(2,128)(2,1)S(1)}, u32[]{:S(2)}, u32[]{:S(2)}) collective-permute-start(bf16[64,1,128]{2,1,0:T(2,128)(2,1)S(1)} %get-tuple-element.54), channel_id=1, source_target_pairs={{0,4},{4,8},{8,12},{1,5},{5,9},{9,13},{2,6},{6,10},{10,14},{3,7},{... | collective-permute-start | bytes 49160 | tf_op jit(solution)/shard_map/ppermute | solution.py:16
  89.0 5.8 %collective-permute-start.9 = (bf16[64,1,128]{2,1,0:T(2,128)(2,1)S(1)}, bf16[64,1,128]{2,1,0:T(2,128)(2,1)S(1)}, u32[]{:S(2)}, u32[]{:S(2)}) collective-permute-start(bf16[64,1,128]{2,1,0:T(2,128)(2,1)S(1)} %get-tuple-element.53), channel_id=1, source_target_pairs={{4,0},{8,4},{12,8},{5,1},{9,5},{13,9},{6,2},{10,6},{14,10},{7,3},{... | collective-permute-start | bytes 49160 | tf_op jit(solution)/shard_map/ppermute | solution.py:18
  94.9 5.1 %collective-permute-start.11 = (bf16[64,10,1]{2,0,1:T(8,128)(2,1)S(1)}, bf16[64,10,1]{2,0,1:T(8,128)(2,1)S(1)}, u32[]{:S(2)}, u32[]{:S(2)}) collective-permute-start(bf16[64,10,1]{2,0,1:T(8,128)(2,1)S(1)} %get-tuple-element.50), channel_id=1, source_target_pairs={{1,0},{2,1},{3,2},{5,4},{6,5},{7,6},{9,8},{10,9},{11,10},{13,12},{... | collective-permute-start | bytes 3848 | tf_op jit(solution)/shard_map/ppermute | solution.py:18
  96.2 4.0 %collective-permute-start.10 = (bf16[64,10,1]{2,0,1:T(8,128)(2,1)S(1)}, bf16[64,10,1]{2,0,1:T(8,128)(2,1)S(1)}, u32[]{:S(2)}, u32[]{:S(2)}) collective-permute-start(bf16[64,10,1]{2,0,1:T(8,128)(2,1)S(1)} %get-tuple-element.49), channel_id=1, source_target_pairs={{0,1},{1,2},{2,3},{4,5},{5,6},{6,7},{8,9},{9,10},{10,11},{12,13},{... | collective-permute-start | bytes 3848 | tf_op jit(solution)/shard_map/ppermute | solution.py:16
Sparse Core Ops, SparseCore 0:
  65.4 20.0 reduce-scatter.1
Sparse Core Ops, SparseCore 1:
  68.8 39.4 all-reduce.6
  112.5 90.1 all-reduce.4
where the time goes:
time: 212 us
  waiting for transfers between devices  131 us (62%)
  starting transfers between devices  27.5 us (13%)
  between operations  16.1 us (8%)
  blocking collectives  13.7 us (6%)
  local copies, waits for them, and re-layouts  8.75 us (4%)
  other arithmetic  7.58 us (4%)
  matrix products  7.49 us (4%)
    psum x1, waiting for transfers between devices, local(): lax.psum(local_one, ('row', 'col', 'pair')) / math.sqrt(height * width)  91.9 us
    ppermute x6, starting transfers between devices, padded_2(): lax.ppermute(tail, axis, [(i, (i + 1) % count) for i in range(ends)])  19.6 us
    reduce_scatter x1, waiting for transfers between devices, local(): lax.psum_scatter(real_columns, 'row', scatter_dimension=2, tiled=True)  18.7 us
    all_gather x1, blocking collectives, local(): column_strip = lax.all_gather(with_edges, 'row', axis=2, tiled=True)  13.7 us
    ppermute x6, waiting for transfers between devices, padded_2(): lax.ppermute(head, axis, [((i + 1) % count, i) for i in range(ends)])  12.2 us
    ppermute x6, starting transfers between devices, padded_2(): lax.ppermute(head, axis, [((i + 1) % count, i) for i in range(ends)])  7.75 us
    psum x1, waiting for transfers between devices, local(): lax.psum(local_two, ('col', 'pair'))  5.73 us
    unnamed x21, local copies, waits for them, and re-layouts  5.7 us
  transfers between devices with their start and end apart: 15, of which 10 were waited for; matrix products, arithmetic and copies ran while one was open for 6% of the time, Pallas kernels for 0%

commit v1 on v0

--- a/solution.py
+++ b/solution.py
@@ -3,6 +3,11 @@
 import jax.numpy as jnp
 from jax import lax
 from jax.sharding import PartitionSpec as P
+
+
+def gather_and_add(x, mesh_axis):
+    parts = lax.all_gather(x, mesh_axis)
+    return jnp.sum(parts, axis=0)
 
 
 def padded_2(cells, sides, width):
@@ -107,7 +112,7 @@
     grad_pooled = lax.psum_scatter(real_columns, "row", scatter_dimension=2, tiled=True)
     grad_pre_one = (unpool_columns(grad_pooled) * silu_slope(pre_one)).astype(jnp.bfloat16)
     local_one = tap_grads(grad_pre_one, padded_in)
-    grad_one = lax.psum(local_one, ("row", "col", "pair")) / math.sqrt(height * width)
+    grad_one = gather_and_add(local_one, ("row", "col", "pair")) / math.sqrt(height * width)
     rimmed_one = padded_2(grad_pre_one, (("row", 1), (("col", "pair"), 2)), 1)
     input_grad = conv_valid(rimmed_one, flip_kernel(filters_one)).astype(jnp.bfloat16)
     return (input_grad, grad_one, grad_two)

time: 212 us -> 156 us (0.74)
  waiting for transfers between devices: 131 us -> 72.3 us
    psum x1 -> x0, waiting for transfers between devices: 91.9 us -> none  [local(): lax.psum(local_one, ('row', 'col', 'pair')) / math.sqrt(height * width)]
    all_gather x0 -> x1, waiting for transfers between devices: none -> 30.2 us  [gather_and_add(): parts = lax.all_gather(x, mesh_axis)]
    reduce_sum x0 -> x1, other arithmetic: none -> 2.93 us  [gather_and_add(): return jnp.sum(parts, axis=0)]
  transfers between devices with their start and end apart: 15 -> 15, of which waited for: 10 -> 11; matrix products, arithmetic and copies ran while one was open for 6% -> 8% of each run, Pallas kernels for 0% -> 0%
where the time goes in v1:
time: 156 us; the launch traced here: 155 us
  waiting for transfers between devices  72.3 us (46%)
  starting transfers between devices  27.7 us (18%)
  between operations  16.1 us (10%)
  blocking collectives  13.7 us (9%)
  other arithmetic  9.55 us (6%)
  local copies, waits for them, and re-layouts  8.38 us (5%)
  matrix products  7.49 us (5%)
    all_gather x1, waiting for transfers between devices, gather_and_add(): parts = lax.all_gather(x, mesh_axis)  30.2 us
    ppermute x6, starting transfers between devices, padded_2(): lax.ppermute(tail, axis, [(i, (i + 1) % count) for i in range(ends)])  19.8 us
    reduce_scatter x1, waiting for transfers between devices, local(): lax.psum_scatter(real_columns, 'row', scatter_dimension=2, tiled=True)  18.7 us
    ppermute x6, waiting for transfers between devices, padded_2(): lax.ppermute(head, axis, [((i + 1) % count, i) for i in range(ends)])  14 us
    all_gather x1, blocking collectives, local(): column_strip = lax.all_gather(with_edges, 'row', axis=2, tiled=True)  13.7 us
    ppermute x6, starting transfers between devices, padded_2(): lax.ppermute(head, axis, [((i + 1) % count, i) for i in range(ends)])  7.75 us
    psum x1, waiting for transfers between devices, local(): lax.psum(local_two, ('col', 'pair'))  6.46 us
    unnamed x21, local copies, waits for them, and re-layouts  5.32 us
  transfers between devices with their start and end apart: 15, of which 11 were waited for; matrix products, arithmetic and copies ran while one was open for 8% of the time, Pallas kernels for 0%

profile of v1, /device:TPU:0, one launch (start us, length us, event | category | flops | bytes accessed | tf_op | source)
XLA Modules:
  0.0 155.2 jit_solution(4527058439460370187)
XLA Ops:
  8.1 1.0 copy.216
  9.1 4.9 %collective-permute-start = (bf16[64,1,128]{2,0,1:T(8,128)(2,1)S(1)}, bf16[64,1,128]{2,0,1:T(8,128)(2,1)S(1)}, u32[]{:S(2)}, u32[]{:S(2)}) collective-permute-start(bf16[64,1,128]{2,0,1:T(8,128)(2,1)S(1)} %get-tuple-element.58), channel_id=1, source_target_pairs={{0,4},{4,8},{8,12},{1,5},{5,9},{9,13},{2,6},{6,10},{10,14},{3,7},{... | collective-permute-start | bytes 49160 | tf_op jit(solution)/shard_map/ppermute | solution.py:21
  14.0 1.3 collective-permute-start.1
  15.4 0.9 constant_dynamic-update-slice_fusion.1
  16.4 3.3 %collective-permute-done.1 = bf16[64,1,128]{2,0,1:T(8,128)(2,1)S(1)} collective-permute-done((bf16[64,1,128]{2,0,1:T(8,128)(2,1)S(1)}, bf16[64,1,128]{2,0,1:T(8,128)(2,1)S(1)}, u32[]{:S(2)}, u32[]{:S(2)}) %collective-permute-start.1) | collective-permute-done | bytes 16416 | tf_op jit(solution)/shard_map/ppermute | solution.py:23
  19.7 1.3 collective-permute-start.3
  21.0 3.0 %collective-permute-start.2 = (bf16[64,10,1]{2,0,1:T(8,128)(2,1)S(1)}, bf16[64,10,1]{2,0,1:T(8,128)(2,1)S(1)}, u32[]{:S(2)}, u32[]{:S(2)}) collective-permute-start(bf16[64,10,1]{2,0,1:T(8,128)(2,1)S(1)} %get-tuple-element.51), channel_id=1, source_target_pairs={{0,1},{1,2},{2,3},{4,5},{5,6},{6,7},{8,9},{9,10},{10,11},{12,13},{... | collective-permute-start | bytes 3848 | tf_op jit(solution)/shard_map/ppermute | solution.py:21
  24.1 1.0 collective-permute-done.2
  25.3 0.3 copy.265
  25.9 0.6 copy-done.3
  26.5 0.8 convolution_select_fusion.1
  27.6 0.9 fusion.3
  28.8 1.3 collective-permute-start.5
  30.1 4.9 %collective-permute-start.4 = (bf16[256,1,2]{1,0,2:T(8,128)(2,1)S(1)}, bf16[256,1,2]{1,0,2:T(8,128)(2,1)S(1)}, u32[]{:S(2)}, u32[]{:S(2)}) collective-permute-start(bf16[256,1,2]{1,0,2:T(8,128)(2,1)S(1)} %get-tuple-element.55), channel_id=1, source_target_pairs={{0,1},{1,2},{2,3},{4,5},{5,6},{6,7},{8,9},{9,10},{10,11},{12,13},{... | collective-permute-start | bytes 3080 | tf_op jit(solution)/shard_map/ppermute | solution.py:21
  35.3 0.7 collective-permute-done.4
  36.2 13.7 %all_gather.9 = bf16[256,34,8]{0,1,2:T(8,128)(2,1)S(1)} all-gather(bf16[256,34,2]{0,1,2:T(8,128)(2,1)S(1)} %copy.226), channel_id=1, replica_groups=mesh['grp'=2,'row'=4,'col'=2,'pair'=2] {'row'}, dimensions={2}, use_global_device_ids=true | all-gather | bytes 174080 | tf_op jit(solution)/shard_map/all_gather | solution.py:97
  50.1 1.0 fusion.6
  52.8 1.0 fusion.4
  53.8 2.5 %collective-permute-start.6 = (f32[256,1,8]{0,2,1:T(8,128)S(1)}, f32[256,1,8]{0,2,1:T(8,128)S(1)}, u32[]{:S(2)}, u32[]{:S(2)}) collective-permute-start(f32[256,1,8]{0,2,1:T(8,128)S(1)} %get-tuple-element.48), channel_id=1, source_target_pairs={{0,1},{1,2},{2,3},{4,5},{5,6},{6,7},{8,9},{9,10},{10,11},{12,13},{... | collective-permute-start | bytes 24584 | tf_op jit(solution)/shard_map/ppermute | solution.py:21
  56.5 1.3 collective-permute-start.7
  57.9 6.6 %collective-permute-done.7 = f32[256,1,8]{0,2,1:T(8,128)S(1)} collective-permute-done((f32[256,1,8]{0,2,1:T(8,128)S(1)}, f32[256,1,8]{0,2,1:T(8,128)S(1)}, u32[]{:S(2)}, u32[]{:S(2)}) %collective-permute-start.7) | collective-permute-done | bytes 8224 | tf_op jit(solution)/shard_map/ppermute | solution.py:23
  64.4 0.8 copy.233
  65.6 1.1 maximum_bitcast_fusion
  66.8 18.7 %reduce-scatter.2.cloned.1.call-done = f32[256,32,2]{0,1,2:T(8,128)} async-done(((f32[256,32,8]{0,1,2:T(8,128)}), f32[256,32,2]{0,1,2:T(8,128)}) %reduce-scatter.2.cloned.1.call-update) | async-done | bytes 65552 | tf_op jit(solution)/shard_map/reduce_scatter | solution.py:112
  85.5 0.8 broadcast_multiply_fusion.2
  87.1 0.3 convolution_bitcast_fusion.9
  87.5 0.2 convolution_bitcast_fusion.11
  87.8 0.3 convolution_bitcast_fusion.15
  88.3 0.2 convolution_bitcast_fusion.17
  88.5 0.3 convolution_bitcast_fusion.12
  88.8 0.3 convolution_bitcast_fusion.14
  89.3 0.7 pad_maximum_fusion
  90.1 1.3 collective-permute-start.8
  91.4 1.3 collective-permute-start.9
  92.7 0.3 collective-permute-done.8
  93.0 4.2 %collective-permute-done.9 = bf16[64,1,128]{2,1,0:T(2,128)(2,1)S(1)} collective-permute-done((bf16[64,1,128]{2,1,0:T(2,128)(2,1)S(1)}, bf16[64,1,128]{2,1,0:T(2,128)(2,1)S(1)}, u32[]{:S(2)}, u32[]{:S(2)}) %collective-permute-start.9) | collective-permute-done | bytes 16416 | tf_op jit(solution)/shard_map/ppermute | solution.py:23
  97.4 1.3 collective-permute-start.11
  98.7 3.2 %collective-permute-start.10 = (bf16[64,10,1]{2,0,1:T(8,128)(2,1)S(1)}, bf16[64,10,1]{2,0,1:T(8,128)(2,1)S(1)}, u32[]{:S(2)}, u32[]{:S(2)}) collective-permute-start(bf16[64,10,1]{2,0,1:T(8,128)(2,1)S(1)} %get-tuple-element.49), channel_id=1, source_target_pairs={{0,1},{1,2},{2,3},{4,5},{5,6},{6,7},{8,9},{9,10},{10,11},{12,13},{... | collective-permute-start | bytes 3848 | tf_op jit(solution)/shard_map/ppermute | solution.py:21
  101.9 0.8 collective-permute-done.10
  102.9 0.3 copy.266
  103.5 0.6 fusion
  104.1 0.9 copy.259
  105.0 6.5 %all-reduce.4.cloned.1.call-done = f32[128,3,3,256]{3,0,1,2:T(8,128)} async-done(((f32[128,3,3,256]{3,0,1,2:T(8,128)}), f32[128,3,3,256]{3,0,1,2:T(8,128)}) %all-reduce.4.cloned.1.call-update) | async-done | bytes 1179664 | tf_op jit(solution)/shard_map/psum | solution.py:105
  111.4 1.4 broadcast_multiply_fusion
  112.8 1.1 copy.260
  113.9 30.2 %all-gather.3.cloned.1.call-done = f32[1024,3,3,64]{3,0,2,1:T(8,128)} async-done(((f32[64,3,3,64]{3,0,2,1:T(8,128)}), f32[1024,3,3,64]{3,0,2,1:T(8,128)}) %all-gather.3.cloned.1.call-update) | async-done | bytes 2359312 | tf_op jit(solution)/shard_map/all_gather | solution.py:9
  144.1 2.9 %reduce_sum.19 = f32[64,3,3,64]{3,0,2,1:T(8,128)S(1)} reduce(f32[16,64,3,3,64]{4,1,0,3,2:T(8,128)} %bitcast.143, f32[]{:T(128)} %constant.68.clone.1), dimensions={0}, to_apply=%region_2.3 | reduce | flops 552960 | bytes 2506756 | tf_op jit(solution)/shard_map/reduce_sum | solution.py:10
  147.0 0.7 broadcast_multiply_fusion.1
  (80 shorter events, 6.4 us)
Async XLA Ops:
  8.0 42.1 %copy-start = (bf16[128,3,3,256]{3,0,2,1:T(8,128)(2,1)S(1)}, bf16[128,3,3,256]{3,0,2,1:T(8,128)(2,1)}, u32[]{:S(2)}) copy-start(bf16[128,3,3,256]{3,0,2,1:T(8,128)(2,1)} %param.10) | copy-start | bytes 1769476
  8.0 77.5 %reduce-scatter.2.cloned.1.call-start = ((), (), s32[]{:S(2)}) async-start(), calls=%async_computation.1 | async-start | bytes 327680 | tf_op jit(solution)/shard_map/reduce_scatter | solution.py:112
  9.1 6.4 %collective-permute-start = (bf16[64,1,128]{2,0,1:T(8,128)(2,1)S(1)}, bf16[64,1,128]{2,0,1:T(8,128)(2,1)S(1)}, u32[]{:S(2)}, u32[]{:S(2)}) collective-permute-start(bf16[64,1,128]{2,0,1:T(8,128)(2,1)S(1)} %get-tuple-element.58), channel_id=1, source_target_pairs={{0,4},{4,8},{8,12},{1,5},{5,9},{9,13},{2,6},{6,10},{10,14},{3,7},{... | collective-permute-start | bytes 49160 | tf_op jit(solution)/shard_map/ppermute | solution.py:21
  14.0 5.6 %collective-permute-start.1 = (bf16[64,1,128]{2,0,1:T(8,128)(2,1)S(1)}, bf16[64,1,128]{2,0,1:T(8,128)(2,1)S(1)}, u32[]{:S(2)}, u32[]{:S(2)}) collective-permute-start(bf16[64,1,128]{2,0,1:T(8,128)(2,1)S(1)} %get-tuple-element.57), channel_id=1, source_target_pairs={{4,0},{8,4},{12,8},{5,1},{9,5},{13,9},{6,2},{10,6},{14,10},{7,3},{... | collective-permute-start | bytes 49160 | tf_op jit(solution)/shard_map/ppermute | solution.py:23
  19.7 4.4 %collective-permute-start.3 = (bf16[64,10,1]{2,0,1:T(8,128)(2,1)S(1)}, bf16[64,10,1]{2,0,1:T(8,128)(2,1)S(1)}, u32[]{:S(2)}, u32[]{:S(2)}) collective-permute-start(bf16[64,10,1]{2,0,1:T(8,128)(2,1)S(1)} %get-tuple-element.52), channel_id=1, source_target_pairs={{1,0},{2,1},{3,2},{5,4},{6,5},{7,6},{9,8},{10,9},{11,10},{13,12},{... | collective-permute-start | bytes 3848 | tf_op jit(solution)/shard_map/ppermute | solution.py:23
  21.0 4.0 %collective-permute-start.2 = (bf16[64,10,1]{2,0,1:T(8,128)(2,1)S(1)}, bf16[64,10,1]{2,0,1:T(8,128)(2,1)S(1)}, u32[]{:S(2)}, u32[]{:S(2)}) collective-permute-start(bf16[64,10,1]{2,0,1:T(8,128)(2,1)S(1)} %get-tuple-element.51), channel_id=1, source_target_pairs={{0,1},{1,2},{2,3},{4,5},{5,6},{6,7},{8,9},{9,10},{10,11},{12,13},{... | collective-permute-start | bytes 3848 | tf_op jit(solution)/shard_map/ppermute | solution.py:21
  25.6 0.9 copy-start.3
  25.6 0.9 copy-start.4
  28.8 6.4 %collective-permute-start.5 = (bf16[256,1,2]{1,0,2:T(8,128)(2,1)S(1)}, bf16[256,1,2]{1,0,2:T(8,128)(2,1)S(1)}, u32[]{:S(2)}, u32[]{:S(2)}) collective-permute-start(bf16[256,1,2]{1,0,2:T(8,128)(2,1)S(1)} %get-tuple-element.56), channel_id=1, source_target_pairs={{1,0},{2,1},{3,2},{5,4},{6,5},{7,6},{9,8},{10,9},{11,10},{13,12},{... | collective-permute-start | bytes 3080 | tf_op jit(solution)/shard_map/ppermute | solution.py:23
  30.1 5.8 %collective-permute-start.4 = (bf16[256,1,2]{1,0,2:T(8,128)(2,1)S(1)}, bf16[256,1,2]{1,0,2:T(8,128)(2,1)S(1)}, u32[]{:S(2)}, u32[]{:S(2)}) collective-permute-start(bf16[256,1,2]{1,0,2:T(8,128)(2,1)S(1)} %get-tuple-element.55), channel_id=1, source_target_pairs={{0,1},{1,2},{2,3},{4,5},{5,6},{6,7},{8,9},{9,10},{10,11},{12,13},{... | collective-permute-start | bytes 3080 | tf_op jit(solution)/shard_map/ppermute | solution.py:21
  50.1 1.0 copy-start.2
  53.8 4.0 %collective-permute-start.6 = (f32[256,1,8]{0,2,1:T(8,128)S(1)}, f32[256,1,8]{0,2,1:T(8,128)S(1)}, u32[]{:S(2)}, u32[]{:S(2)}) collective-permute-start(f32[256,1,8]{0,2,1:T(8,128)S(1)} %get-tuple-element.48), channel_id=1, source_target_pairs={{0,1},{1,2},{2,3},{4,5},{5,6},{6,7},{8,9},{9,10},{10,11},{12,13},{... | collective-permute-start | bytes 24584 | tf_op jit(solution)/shard_map/ppermute | solution.py:21
  56.5 7.9 %collective-permute-start.7 = (f32[256,1,8]{0,2,1:T(8,128)S(1)}, f32[256,1,8]{0,2,1:T(8,128)S(1)}, u32[]{:S(2)}, u32[]{:S(2)}) collective-permute-start(f32[256,1,8]{0,2,1:T(8,128)S(1)} %get-tuple-element.47), channel_id=1, source_target_pairs={{1,0},{2,1},{3,2},{5,4},{6,5},{7,6},{9,8},{10,9},{11,10},{13,12},{... | collective-permute-start | bytes 24584 | tf_op jit(solution)/shard_map/ppermute | solution.py:23
  65.2 46.2 %all-reduce.4.cloned.1.call-start = ((), (), s32[]{:S(2)}) async-start(), calls=%async_computation.2 | async-start | bytes 2359296 | tf_op jit(solution)/shard_map/psum | solution.py:105
  66.8 77.3 %all-gather.3.cloned.1.call-start = ((), (), s32[]{:S(2)}) async-start(), calls=%async_computation.3 | async-start | bytes 5013504 | tf_op jit(solution)/shard_map/all_gather | solution.py:9
  88.1 1.0 copy-start.1
  90.1 2.9 %collective-permute-start.8 = (bf16[64,1,128]{2,1,0:T(2,128)(2,1)S(1)}, bf16[64,1,128]{2,1,0:T(2,128)(2,1)S(1)}, u32[]{:S(2)}, u32[]{:S(2)}) collective-permute-start(bf16[64,1,128]{2,1,0:T(2,128)(2,1)S(1)} %get-tuple-element.54), channel_id=1, source_target_pairs={{0,4},{4,8},{8,12},{1,5},{5,9},{9,13},{2,6},{6,10},{10,14},{3,7},{... | collective-permute-start | bytes 49160 | tf_op jit(solution)/shard_map/ppermute | solution.py:21
  91.4 5.8 %collective-permute-start.9 = (bf16[64,1,128]{2,1,0:T(2,128)(2,1)S(1)}, bf16[64,1,128]{2,1,0:T(2,128)(2,1)S(1)}, u32[]{:S(2)}, u32[]{:S(2)}) collective-permute-start(bf16[64,1,128]{2,1,0:T(2,128)(2,1)S(1)} %get-tuple-element.53), channel_id=1, source_target_pairs={{4,0},{8,4},{12,8},{5,1},{9,5},{13,9},{6,2},{10,6},{14,10},{7,3},{... | collective-permute-start | bytes 49160 | tf_op jit(solution)/shard_map/ppermute | solution.py:23
  97.4 4.5 %collective-permute-start.11 = (bf16[64,10,1]{2,0,1:T(8,128)(2,1)S(1)}, bf16[64,10,1]{2,0,1:T(8,128)(2,1)S(1)}, u32[]{:S(2)}, u32[]{:S(2)}) collective-permute-start(bf16[64,10,1]{2,0,1:T(8,128)(2,1)S(1)} %get-tuple-element.50), channel_id=1, source_target_pairs={{1,0},{2,1},{3,2},{5,4},{6,5},{7,6},{9,8},{10,9},{11,10},{13,12},{... | collective-permute-start | bytes 3848 | tf_op jit(solution)/shard_map/ppermute | solution.py:23
  98.7 4.0 %collective-permute-start.10 = (bf16[64,10,1]{2,0,1:T(8,128)(2,1)S(1)}, bf16[64,10,1]{2,0,1:T(8,128)(2,1)S(1)}, u32[]{:S(2)}, u32[]{:S(2)}) collective-permute-start(bf16[64,10,1]{2,0,1:T(8,128)(2,1)S(1)} %get-tuple-element.49), channel_id=1, source_target_pairs={{0,1},{1,2},{2,3},{4,5},{5,6},{6,7},{8,9},{9,10},{10,11},{12,13},{... | collective-permute-start | bytes 3848 | tf_op jit(solution)/shard_map/ppermute | solution.py:21
Sparse Core Ops, SparseCore 0:
  65.4 20.0 reduce-scatter.1
  90.2 53.8 all-gather.2
Sparse Core Ops, SparseCore 1:
  68.8 42.6 all-reduce.3
